TPU v7x, 256 devices: a whole 4x4x8 slice. The times are simulated.
256 devices in a mesh: batch: 8 (over y, core), proto: 32 (over z, x).
Axes of the slice: x: 4, y: 4, z: 8, core: 2. Of those that a mesh axis runs over, the one named last changes fastest.
Arguments:
- student_codes: bfloat16 [8192, 256], P(('batch', 'proto')), may hold values from -2.5 to 2.5
- teacher_codes: bfloat16 [8192, 256], P(('batch', 'proto')), may hold values from -2.5 to 2.5
- prototypes: float32 [256, 65536], P(None, 'proto'), may hold values from -48 to 48
Outputs:
- proto_grad: float32 [256, 65536], P('batch', 'proto')
- loss_rows: float32 [8192], P(('batch', 'proto'))
All inputs are finite; a program needn't handle non-finite values.
Results may differ from a plain program's by a relative error of at most 0.0009.
The roundings to bfloat16 on the way count: a program that leaves them out, or rounds other values in their place, can miss the bound.
Values may be sent and summed in bfloat16 or wider, within the bound.
No kernel may reach another device: no remote copies, remote signals or barrier semaphores. Data moves between devices by JAX's collectives and lax.ppermute only.
A program may use at most 64 MiB of HBM per device.

v0:
```python
import functools

import jax
import jax.numpy as jnp
from jax import lax
from jax.experimental import pallas as pl
from jax.experimental.pallas import tpu as pltpu
from jax.sharding import Mesh, PartitionSpec as P

ITERS = 3

student_temp = 0.1
teacher_temp = 0.07
norm_eps = 1e-06
log2_e = 1.4426950408889634

BATCH = ("y", "core")
PROTO = ("z", "x")
BATCHES = 8
PROTOS = 32
ROWS = 1024
COLS = 2048
WIDTH = 256
LANES = 128
ROW_TILES = ROWS // LANES
COL_TILES = COLS // LANES
CHUNK = 256
WIDE = 512
HALF = COLS // 2
HEAD = 14.0
FLAT = ROWS + LANES
OWN = ROWS // PROTOS
ZS = 8
XS = 4
BLOCK = ROWS // XS
f32 = jnp.float32
bf16 = jnp.bfloat16


def unit_rows(values):
    values = values.astype(f32)
    return values * lax.rsqrt(jnp.sum(values * values, axis=-1, keepdims=True) + norm_eps)


def row_of_lane_sums(parts_ref, out_row, pieces=ROW_TILES):
    for g in range(pieces):
        block = parts_ref[pl.ds(g * LANES, LANES), :]
        out_row(g, jnp.sum(block.T, axis=0, keepdims=True))


def column_of_row(row, out_ref):
    for g in range(ROW_TILES):
        out_ref[pl.ds(g * LANES, LANES), :] = jnp.broadcast_to(row[g : g + 1, :], (LANES, LANES)).T


def spread_columns(column_mass, pay_ref):
    row = jnp.concatenate([column_mass[:, t * LANES : (t + 1) * LANES] for t in range(COL_TILES)], axis=0)
    for k in range(BATCHES):
        pay_ref[k] = row


def block_place(q):
    step = lax.rem(q // 2 - lax.axis_index("y") + 4, 4)
    return jnp.where(lax.axis_index("core") == q % 2, 0, 4) + step


def block_rows(p):
    row = lax.rem(lax.axis_index("y") + p % 4, 4)
    core = lax.axis_index("core")
    return 2 * row + (core if p < 4 else 1 - core)


def owned_piece(row, k):
    z, x = k // XS, k % XS
    line = 2 * x + z // 4
    return pltpu.roll(row[line : line + 1, :], (LANES - (z % 4) * OWN) % LANES, 1)


def flat_row(row):
    return jnp.concatenate([row[g : g + 1, :] for g in range(ROW_TILES)], axis=1)


def flat_rows(flat):
    return jnp.concatenate([flat[:, g * LANES : (g + 1) * LANES] for g in range(ROW_TILES)], axis=0)


def copy_kernel(teacher_hbm, student_hbm, pay_ref, codes_ref, sems):
    copies = [
        pltpu.make_async_copy(teacher_hbm, codes_ref.at[0], sems.at[0]),
        pltpu.make_async_copy(student_hbm, codes_ref.at[1], sems.at[1]),
    ]
    for copy in copies:
        copy.start()
    for copy in copies:
        copy.wait()
    for t in range(2):
        unit = unit_rows(codes_ref[t]).astype(bf16)
        for k in range(ZS):
            pay_ref[k, pl.ds(t * OWN, OWN), :] = unit


def split_kernel(came_ref, teacher_ref, student_ref):
    teacher_ref[...] = came_ref[:, 0:OWN, :].reshape(BLOCK, WIDTH)
    student_ref[...] = came_ref[:, OWN : 2 * OWN, :].reshape(BLOCK, WIDTH)


def norm_kernel(proto_hbm, after_ref, low_ref, inverse_ref, proto_ref, sems):
    copies = [
        pltpu.make_async_copy(proto_hbm.at[:, pl.ds(j, WIDE)], proto_ref.at[:, pl.ds(j, WIDE)], sems.at[j // WIDE])
        for j in range(0, COLS, WIDE)
    ]
    for copy in copies:
        copy.start()
    for j in range(0, COLS, WIDE):
        copies[j // WIDE].wait()
        cols = pl.ds(j, WIDE)
        piece = proto_ref[:, cols]
        inverse = lax.rsqrt(jnp.sum(piece * piece, axis=0, keepdims=True) + norm_eps)
        inverse_ref[:, cols] = inverse
        low_ref[:, cols] = (piece * inverse).astype(bf16)


def block_starts():
    x = lax.axis_index("x")
    return [pl.multiple_of(lax.rem(x + XS - k, XS) * BLOCK, BLOCK) for k in range(XS)]


def teacher_kernel(u0_ref, u1_ref, u2_ref, u3_ref, low_ref, weights_ref, mass_ref):
    units, starts = (u0_ref, u1_ref, u2_ref, u3_ref), block_starts()

    for j in range(0, COLS, WIDE):
        cols = pl.ds(j, WIDE)
        low = low_ref[:, cols]
        mass = jnp.zeros((8, WIDE), f32)
        for unit_ref, start in zip(units, starts):
            scores = jnp.dot(unit_ref[...], low, preferred_element_type=f32)
            weights = jnp.exp2(scores * (log2_e / teacher_temp))
            weights_ref[pl.ds(start, BLOCK), cols] = weights
            mass = mass + jnp.sum(weights.reshape(BLOCK // 8, 8, WIDE), axis=0)
        mass_ref[:, cols] = jnp.sum(mass, axis=0, keepdims=True)


def student_kernel(
    u0_ref,
    u1_ref,
    u2_ref,
    u3_ref,
    low_ref,
    mass_ref,
    scores_ref,
    exp_ref,
    unit_t_ref,
    total_ref,
    pay_ref,
    parts_ref,
):
    units, starts = (u0_ref, u1_ref, u2_ref, u3_ref), block_starts()
    place = [pl.multiple_of(block_place(q) * 32, 32) for q in range(8)]
    for unit_ref, start in zip(units, starts):
        turned = unit_ref[...].astype(f32).T.astype(bf16)
        for q in range(8):
            unit_t_ref[pl.ds(place[q], 32), pl.ds(start, BLOCK)] = turned[q * 32 : q * 32 + 32, :]
    parts_ref[...] = jnp.zeros_like(parts_ref)

    for j in range(0, COLS, WIDE):
        cols = pl.ds(j, WIDE)
        low = low_ref[:, cols]
        for unit_ref, start in zip(units, starts):
            rows = pl.ds(start, BLOCK)
            scores = jnp.dot(unit_ref[...], low, preferred_element_type=f32)
            scores_ref[rows, cols] = scores
            grown = jnp.exp2(scores * (log2_e / student_temp))
            exp_ref[rows, cols] = grown
            parts_ref[rows, :] += sum(grown[:, t : t + LANES] for t in range(LANES, WIDE, LANES)) + grown[:, :LANES]

    spread_columns(mass_ref[...], pay_ref)

    def put(g, row):
        total_ref[g : g + 1, :] = row

    row_of_lane_sums(parts_ref, put)


def scaled_rows(column, weights_ref, parts_ref, scores_ref=None, cross_ref=None):
    scale = [jnp.broadcast_to(column[t : t + 1, :], (8, LANES)) for t in range(COL_TILES)]

    for i in range(0, ROWS, 8):
        rows = pl.ds(i, 8)
        mass = cross = None
        for t in range(COL_TILES):
            cols = pl.ds(t * LANES, LANES)
            term = weights_ref[rows, cols] * scale[t]
            mass = term if mass is None else mass + term
            if scores_ref is not None:
                term = term * scores_ref[rows, cols]
                cross = term if cross is None else cross + term
        parts_ref[rows, :] = mass
        if scores_ref is not None:
            cross_ref[rows, :] = cross


def row_kernel(spread, mass_ref, weights_ref, extra_ref, pay_ref, parts_ref, row_ref):
    scaled_rows(1.0 / jnp.sum(mass_ref[...], axis=0), weights_ref, parts_ref)

    def put(g, row):
        row_ref[g : g + 1, :] = row

    row_of_lane_sums(parts_ref, put)
    flat, extra = flat_row(row_ref[...]), extra_ref[...]
    for k in range(PROTOS):
        pay_ref[k, :, 0:ROWS] = flat
        pay_ref[k, :, ROWS:FLAT] = owned_piece(extra, k) if spread else extra


def last_row_kernel(mass_ref, weights_ref, scores_ref, pay_ref, column_ref, parts_ref, cross_ref, row_ref):
    column = 1.0 / jnp.sum(mass_ref[...], axis=0)
    column_ref[...] = column
    scaled_rows(column, weights_ref, parts_ref, scores_ref, cross_ref)

    def put_mass(g, row):
        row_ref[g : g + 1, :] = row

    def put_cross(g, row):
        row_ref[ROW_TILES + g : ROW_TILES + g + 1, :] = row

    row_of_lane_sums(parts_ref, put_mass)
    row_of_lane_sums(cross_ref, put_cross)
    flat, cross = flat_row(row_ref[0:ROW_TILES, :]), row_ref[ROW_TILES : 2 * ROW_TILES, :]
    for k in range(PROTOS):
        pay_ref[k, :, 0:ROWS] = flat
        pay_ref[k, :, ROWS:FLAT] = owned_piece(cross, k)


def column_kernel(gather, mass_ref, weights_ref, pay_ref, extra_ref, scale_ref, sums_ref):
    sums = jnp.sum(mass_ref[...], axis=0)
    column_of_row(1.0 / flat_rows(sums), scale_ref)
    if gather:
        lane = lax.broadcasted_iota(jnp.int32, (1, LANES), 1)
        for g in range(ROW_TILES):
            row = jnp.zeros((1, LANES), f32)
            for t in range(4):
                piece = jnp.where(lane < OWN, mass_ref[(4 * (g % 2) + t) * XS + g // 2, :, ROWS:FLAT], 0.0)
                row = row + (pltpu.roll(piece, t * OWN, 1) if t else piece)
            extra_ref[g : g + 1, :] = row
    else:
        extra_ref[...] = sums[:, ROWS:FLAT]

    sums = [jnp.zeros((8, LANES), f32)] * COL_TILES
    for i in range(0, ROWS, 8):
        rows = pl.ds(i, 8)
        scale = scale_ref[rows, :]
        for t in range(COL_TILES):
            sums[t] = sums[t] + weights_ref[rows, pl.ds(t * LANES, LANES)] * scale
    for t in range(COL_TILES):
        sums_ref[t : t + 1, :] = jnp.sum(sums[t], axis=0, keepdims=True)
    row = sums_ref[...]
    for k in range(BATCHES):
        pay_ref[k] = row


def grad_columns(half, weights_ref, exp_ref, column_ref, unit_t_ref, proto_ref, inverse_ref, prob_ref, target_ref, outs):
    kept_ref, sent_ref = outs
    blocks = [pl.multiple_of(block_rows(p) * 32, 32) for p in range(8)]
    for j in range(0, HALF, CHUNK):
        cols = pl.ds(half * HALF + j, CHUNK)
        pieces = []
        for t in range(half * HALF + j, half * HALF + j + CHUNK, LANES):
            part = pl.ds(t, LANES)
            scale = column_ref[t // LANES : t // LANES + 1, :]
            pieces.append(
                (exp_ref[:, part] * prob_ref[...] - weights_ref[:, part] * scale * target_ref[...]).astype(bf16)
            )
        score_grad = jnp.concatenate(pieces, axis=1)
        grad = jnp.dot(unit_t_ref[...], score_grad, preferred_element_type=f32)
        inverse = inverse_ref[:, cols]
        directions = jnp.concatenate([proto_ref[pl.ds(b, 32), cols] for b in blocks], axis=0) * inverse
        radial = jnp.sum(directions * grad, axis=0, keepdims=True)
        full = (grad - directions * radial) * inverse
        for s in range(4):
            kept_ref[s, :, pl.ds(j, CHUNK)] = full[s * 32 : s * 32 + 32, :]
            sent_ref[s, :, pl.ds(j, CHUNK)] = full[128 + s * 32 : 160 + s * 32, :]


def first_grad_kernel(
    mass_ref,
    total_ref,
    weights_ref,
    exp_ref,
    column_ref,
    unit_t_ref,
    proto_ref,
    inverse_ref,
    kept_ref,
    sent_ref,
    prob_ref,
    target_ref,
    own_ref,
    row_ref,
):
    sums = jnp.sum(mass_ref[...], axis=0)
    row_ref[...] = 1.0 / flat_rows(sums)
    factor = 1.0 / (student_temp * ROWS * BATCHES)
    column_of_row(factor / total_ref[...], prob_ref)
    column_of_row(factor * row_ref[...], target_ref)
    z = lax.axis_index("z")
    line, turn = pl.ds(2 * lax.axis_index("x") + z // 4, 1), LANES - lax.rem(z, 4) * OWN
    row_scale = pltpu.roll(row_ref[line, :], turn, 1)
    total = pltpu.roll(total_ref[line, :], turn, 1)
    own_ref[...] = jnp.log(total) - sums[:, ROWS:FLAT] * row_scale * (1.0 / student_temp)
    tables = (weights_ref, exp_ref, column_ref, unit_t_ref, proto_ref, inverse_ref)
    grad_columns(0, *tables, prob_ref, target_ref, (kept_ref, sent_ref))


def second_grad_kernel(*refs):
    grad_columns(1, *refs[:8], refs[8:])


def pair_kernel(kept_ref, came_ref, own_ref, *out_refs):
    for s, out_ref in zip((2, 1, 3), out_refs):
        exponents = []
        for t in range(HALF // LANES):
            cols = pl.ds(t * LANES, LANES)
            value = kept_ref[s, :, cols] + came_ref[s, :, cols]
            top = jnp.max(jnp.abs(value), axis=0, keepdims=True)
            exponent = jnp.clip(jnp.ceil(jnp.log2(top)), -100.0, 120.0)
            out_ref[:, cols] = value * jnp.exp2(HEAD - exponent)
            exponents.append(exponent)
        out_ref[0:8, HALF:] = jnp.concatenate(exponents, axis=0)
        out_ref[8:32, HALF:] = jnp.zeros((24, LANES), f32)
    own_ref[...] = kept_ref[0] + came_ref[0]


def sum_kernel(*refs):
    out_ref = refs[-1]
    for half in range(2):
        own_ref, *block_refs = refs[4 * half : 4 * half + 4]
        scales = [jnp.exp2(ref[0:8, HALF:] - HEAD) for ref in block_refs]
        for t in range(HALF // LANES):
            cols = pl.ds(t * LANES, LANES)
            value = own_ref[:, cols]
            for ref, scale in zip(block_refs, scales):
                value = value + ref[:, cols] * scale[t : t + 1, :]
            out_ref[:, pl.ds(half * HALF + t * LANES, LANES)] = value


def call(kernel, outs, scratch, homes):
    spaces = {"v": pltpu.VMEM, "h": pltpu.HBM}

    def shape(out):
        dims, dtype, kept = out
        return pltpu.VMEM(dims, dtype) if kept else jax.ShapeDtypeStruct(dims, dtype)

    def run(*operands):
        placed = [
            pltpu.with_memory_space_constraint(x, spaces[h]) if h in spaces else x for x, h in zip(operands, homes)
        ]
        return pl.pallas_call(
            kernel,
            out_shape=[shape(o) for o in outs],
            in_specs=[pl.BlockSpec(memory_space=pl.ANY if h == "h" else pltpu.VMEM) for h in homes],
            out_specs=[pl.BlockSpec(memory_space=pltpu.VMEM if o[2] is not None else pl.ANY) for o in outs],
            scratch_shapes=scratch,
            compiler_params=pltpu.CompilerParams(vmem_limit_bytes=12 * 2**20),
            cost_estimate=pl.CostEstimate(flops=0, bytes_accessed=0, transcendentals=0),
        )(*placed)

    return run


def share(value, axes, count):
    return lax.all_to_all(value, axes, 0, 0, tiled=True)


def shift(value, step, axis="y"):
    return lax.ppermute(value, axis, [(i, (i + step) % 4) for i in range(4)])


def scatter_half(kept, sent):
    came = lax.ppermute(sent, "core", [(0, 1), (1, 0)])
    out = ((32, HALF + LANES), f32, True)
    own, *blocks = call(pair_kernel, [((32, HALF), f32, True), out, out, out], [], "vv")(kept, came)
    return [own] + [shift(block.astype(jnp.float16), k).astype(f32) for block, k in zip(blocks, (2, 1, 3))]


def on_device(student_codes, teacher_codes, prototypes):
    table, column = ((ROWS, COLS), f32, True), ((COL_TILES, LANES), f32, True)
    to_batch, to_proto = ((BATCHES, COL_TILES, LANES), f32, True), ((PROTOS, 1, FLAT), f32, True)
    crops, owned = ((ROW_TILES, LANES), f32, True), ((1, LANES), f32, True)
    lanes, row = pltpu.VMEM((ROWS, LANES), f32), pltpu.VMEM((ROW_TILES, LANES), f32)
    (pay,) = call(
        copy_kernel,
        [((ZS, 2 * OWN, WIDTH), bf16, True)],
        [pltpu.VMEM((2, OWN, WIDTH), bf16), pltpu.SemaphoreType.DMA((2,))],
        "hh",
    )(teacher_codes, student_codes)
    block, inverse_row = ((BLOCK, WIDTH), bf16, True), ((1, COLS), f32, True)
    teacher, student = call(split_kernel, [block, block], [], "v")(share(pay, "z", ZS))
    low, inverse, protos = call(
        norm_kernel,
        [((WIDTH, COLS), bf16, True), inverse_row, ((WIDTH, COLS), f32, True)],
        [pltpu.SemaphoreType.DMA((COLS // WIDE,))],
        "hv",
    )(prototypes, teacher)
    teachers = [teacher] + [shift(teacher, k, "x") for k in (1, 2, 3)]
    above = shift(student, 3, "x")
    students = [student, shift(student, 1, "x"), shift(above, 3, "x"), above]
    weights, mass = call(teacher_kernel, [table, inverse_row], [], "vvvvv")(*teachers, low)
    scores, grown, unit_t, extra, pay = call(
        student_kernel, [table, table, ((WIDTH, ROWS), bf16, True), crops, to_batch], [lanes], "vvvvvv"
    )(*students, low, mass)
    for iteration in range(ITERS - 1):
        first = iteration == 0
        (pay,) = call(functools.partial(row_kernel, first), [to_proto], [lanes, row], "vvv")(
            share(pay, BATCH, BATCHES), weights, extra
        )
        pay, extra = call(
            functools.partial(column_kernel, not first),
            [to_batch, owned if first else crops],
            [lanes, pltpu.VMEM((COL_TILES, LANES), f32)],
            "vv",
        )(share(pay, PROTO, PROTOS), weights)
    pay, column_scale = call(
        last_row_kernel,
        [to_proto, column],
        [lanes, lanes, pltpu.VMEM((2 * ROW_TILES, LANES), f32)],
        "vvv",
    )(share(pay, BATCH, BATCHES), weights, scores)
    part, whole = ((4, 32, HALF), f32, True), ((ROWS, LANES), f32, True)
    tables = (weights, grown, column_scale, unit_t, protos, inverse)
    kept, sent, prob, target, own = call(
        first_grad_kernel, [part, part, whole, whole, ((1, LANES), f32, False)], [row], "vvvvvvvv"
    )(share(pay, PROTO, PROTOS), extra, *tables)
    first = scatter_half(kept, sent)
    kept, sent = call(second_grad_kernel, [part, part], [], "vvvvvvvv")(*tables, prob, target)
    second = scatter_half(kept, sent)
    (out,) = call(sum_kernel, [((32, COLS), f32, False)], [], "vvvvvvvv")(*first, *second)
    return (out, own[0, :OWN])


def solution(mesh):
    fine = Mesh(mesh.devices.reshape(4, 2, 8, 4), BATCH + PROTO)
    rows = P(BATCH + PROTO, None)
    return jax.shard_map(
        on_device,
        mesh=fine,
        in_specs=(rows, rows, P(None, PROTO)),
        out_specs=(P(BATCH, PROTO), P(BATCH + PROTO)),
        check_vma=False,
    )
```

profile of v0, /device:TPU:8, one launch (start us, length us, event | category | flops | bytes accessed | tf_op | source)
XLA Modules:
  0.0 128.2 jit_solution(11448842611664556340)
XLA Ops:
  0.6 0.9 shard_map.50
  1.5 20.1 %all_to_all.35.came_ref = bf16[8,64,256]{2,1,0:T(8,128)(2,1)S(1)} all-to-all(bf16[8,64,256]{2,1,0:T(8,128)(2,1)S(1)} %shard_map.50), channel_id=1, replica_groups=mesh['y'=4,'core'=2,'z'=8,'x'=4] {'z'}, dimensions={0} | all-to-all | bytes 524288 | tf_op jit(solution)/shard_map/all_to_all | solution.py:371
  21.7 2.8 %collective-permute-start.1 = (bf16[256,256]{1,0:T(8,128)(2,1)S(1)}, bf16[256,256]{1,0:T(8,128)(2,1)S(1)}, u32[]{:S(2)}, u32[]{:S(2)}) collective-permute-start(bf16[256,256]{1,0:T(8,128)(2,1)S(1)} %get-tuple-element.35.u0_ref), channel_id=1, source_target_pairs={{0,3},{1,0},{2,1},{3,2},{4,7},{5,4},{6,5},{7,6},{8,11},{9,8},{10,9... | collective-permute-start | bytes 393224 | tf_op jit(solution)/shard_map/ppermute | solution.py:375
  24.5 0.8 collective-permute-start.5
  25.3 0.5 collective-permute-start.4
  25.8 0.9 collective-permute-start.3
  26.7 2.1 %collective-permute-start = (bf16[256,256]{1,0:T(8,128)(2,1)S(1)}, bf16[256,256]{1,0:T(8,128)(2,1)S(1)}, u32[]{:S(2)}, u32[]{:S(2)}) collective-permute-start(bf16[256,256]{1,0:T(8,128)(2,1)S(1)} %get-tuple-element.35.u0_ref), channel_id=1, source_target_pairs={{0,1},{1,2},{2,3},{3,0},{4,5},{5,6},{6,7},{7,4},{8,9},{9,10},{10,1... | collective-permute-start | bytes 393224 | tf_op jit(solution)/shard_map/ppermute | solution.py:375
  28.8 0.0 collective-permute-done.1.u3_ref
  28.8 2.6 %collective-permute-start.2 = (bf16[256,256]{1,0:T(8,128)(2,1)S(1)}, bf16[256,256]{1,0:T(8,128)(2,1)S(1)}, u32[]{:S(2)}, u32[]{:S(2)}) collective-permute-start(bf16[256,256]{1,0:T(8,128)(2,1)S(1)} %collective-permute-done.1.u3_ref), channel_id=1, source_target_pairs={{0,3},{1,0},{2,1},{3,2},{4,7},{5,4},{6,5},{7,6},{8,11},{9,8},{10,9... | collective-permute-start | bytes 393224 | tf_op jit(solution)/shard_map/ppermute | solution.py:375
  31.5 1.6 %shard_map.52 = (bf16[256,2048]{1,0:T(8,128)(2,1)S(1)}, f32[1,2048]{1,0:T(1,128)S(1)}, f32[256,2048]{1,0:T(8,128)S(1)}) custom-call(f32[256,2048]{1,0:T(8,128)} %proto_hbm.1, bf16[256,256]{1,0:T(8,128)(2,1)S(1)} %get-tuple-element.36.after_ref.u0_ref), custom_call_target="tpu_custom_call" | custom-call | tf_op jit(solution)/shard_map/pallas_call | solution.py:357
  33.1 0.0 collective-permute-done.5.u3_ref
  33.1 0.0 collective-permute-done.4.u2_ref
  33.1 0.8 collective-permute-done.3.u1_ref
  33.9 1.3 shard_map.53
  35.2 0.1 collective-permute-done.u1_ref
  35.3 0.0 collective-permute-done.2.u2_ref
  35.3 1.8 %shard_map.54 = (f32[1024,2048]{1,0:T(8,128)S(1)}, f32[1024,2048]{1,0:T(8,128)S(1)}, bf16[256,1024]{1,0:T(8,128)(2,1)S(1)}, f32[8,128]{1,0:T(8,128)S(1)}, f32[8,16,128]{2,1,0:T(8,128)S(1)}) custom-call(bf16[256,256]{1,0:T(8,128)(2,1)S(1)} %get-tuple-element.35.u0_ref, bf16[256,256]{1,0:T(8,128)(2,1)S(1)} %collective-permute-done.u1_ref, ...), custom_call_target="tpu_custom_call" | custom-call | tf_op jit(solution)/shard_map/pallas_call | solution.py:357
  37.1 8.9 %all_to_all.36.mass_ref = f32[8,16,128]{2,1,0:T(8,128)S(1)} all-to-all(f32[8,16,128]{2,1,0:T(8,128)S(1)} %get-tuple-element.39), channel_id=1, replica_groups=mesh['y'=4,'core'=2,'z'=8,'x'=4] {'y','core'}, dimensions={0} | all-to-all | bytes 131072 | tf_op jit(solution)/shard_map/all_to_all | solution.py:371
  46.0 0.7 shard_map.55
  46.7 15.9 %all_to_all.37.mass_ref = f32[32,1,1152]{2,1,0:T(1,128)S(1)} all-to-all(f32[32,1,1152]{2,1,0:T(1,128)S(1)} %shard_map.55), channel_id=1, replica_groups=mesh['y'=4,'core'=2,'z'=8,'x'=4] {'z','x'}, dimensions={0} | all-to-all | bytes 294912 | tf_op jit(solution)/shard_map/all_to_all | solution.py:371
  62.6 0.8 shard_map.56
  63.4 8.0 %all_to_all.38.mass_ref = f32[8,16,128]{2,1,0:T(8,128)S(1)} all-to-all(f32[8,16,128]{2,1,0:T(8,128)S(1)} %get-tuple-element.42), channel_id=1, replica_groups=mesh['y'=4,'core'=2,'z'=8,'x'=4] {'y','core'}, dimensions={0} | all-to-all | bytes 131072 | tf_op jit(solution)/shard_map/all_to_all | solution.py:371
  71.4 0.6 shard_map.57
  72.1 14.0 %all_to_all.39.mass_ref = f32[32,1,1152]{2,1,0:T(1,128)S(1)} all-to-all(f32[32,1,1152]{2,1,0:T(1,128)S(1)} %shard_map.57), channel_id=1, replica_groups=mesh['y'=4,'core'=2,'z'=8,'x'=4] {'z','x'}, dimensions={0} | all-to-all | bytes 294912 | tf_op jit(solution)/shard_map/all_to_all | solution.py:371
  86.1 0.8 shard_map.58
  86.9 8.0 %all_to_all.40.mass_ref = f32[8,16,128]{2,1,0:T(8,128)S(1)} all-to-all(f32[8,16,128]{2,1,0:T(8,128)S(1)} %get-tuple-element.44), channel_id=1, replica_groups=mesh['y'=4,'core'=2,'z'=8,'x'=4] {'y','core'}, dimensions={0} | all-to-all | bytes 131072 | tf_op jit(solution)/shard_map/all_to_all | solution.py:371
  94.9 1.8 %shard_map.59 = (f32[32,1,1152]{2,1,0:T(1,128)S(1)}, f32[16,128]{1,0:T(8,128)S(1)}) custom-call(f32[8,16,128]{2,1,0:T(8,128)S(1)} %all_to_all.40.mass_ref, f32[1024,2048]{1,0:T(8,128)S(1)} %get-tuple-element.40.weights_ref.refs_0_, f32[1024,2048]{1,0:T(8,128)S(1)} %get-tuple-element.45.scores_ref), custom_call_target="tpu_custom_call" | custom-call | tf_op jit(solution)/shard_map/pallas_call | solution.py:357
  96.7 14.0 %all_to_all.41.mass_ref = f32[32,1,1152]{2,1,0:T(1,128)S(1)} all-to-all(f32[32,1,1152]{2,1,0:T(1,128)S(1)} %get-tuple-element.46), channel_id=1, replica_groups=mesh['y'=4,'core'=2,'z'=8,'x'=4] {'z','x'}, dimensions={0} | all-to-all | bytes 294912 | tf_op jit(solution)/shard_map/all_to_all | solution.py:371
  110.8 1.5 %shard_map.60 = (f32[4,32,1024]{2,1,0:T(8,128)S(1)}, f32[4,32,1024]{2,1,0:T(8,128)S(1)}, f32[1024,128]{1,0:T(8,128)S(1)}, f32[1024,128]{1,0:T(8,128)S(1)}, f32[1,128]{1,0:T(1,128)S(1)}) custom-call(f32[32,1,1152]{2,1,0:T(1,128)S(1)} %all_to_all.41.mass_ref, f32[8,128]{1,0:T(8,128)S(1)} %get-tuple-element.47.total_ref, ...), custom_call_target="tpu_custom_call" | custom-call | tf_op jit(solution)/shard_map/pallas_call | solution.py:357
  112.3 0.1 collective-permute-start.6
  112.4 1.2 shard_map.62
  113.6 0.6 collective-permute-start.10
  114.1 0.1 collective-permute-done.6.came_ref
  114.3 0.1 shard_map.61
  114.4 1.5 %collective-permute-start.9 = (f16[32,1152]{1,0:T(8,128)(2,1)S(1)}, f16[32,1152]{1,0:T(8,128)(2,1)S(1)}, u32[]{:S(2)}, u32[]{:S(2)}) collective-permute-start(f16[32,1152]{1,0:T(8,128)(2,1)S(1)} %convert_element_type.40), channel_id=1, source_target_pairs={{0,192},{64,0},{128,64},{192,128},{1,193},{65,1},{129,65},{193,129... | collective-permute-start | bytes 221192 | tf_op jit(solution)/shard_map/ppermute | solution.py:375
  115.9 0.6 collective-permute-start.8
  116.6 2.7 %collective-permute-start.7 = (f16[32,1152]{1,0:T(8,128)(2,1)S(1)}, f16[32,1152]{1,0:T(8,128)(2,1)S(1)}, u32[]{:S(2)}, u32[]{:S(2)}) collective-permute-start(f16[32,1152]{1,0:T(8,128)(2,1)S(1)} %convert_element_type.36), channel_id=1, source_target_pairs={{0,128},{64,192},{128,0},{192,64},{1,129},{65,193},{129,1},{193,65... | collective-permute-start | bytes 221192 | tf_op jit(solution)/shard_map/ppermute | solution.py:375
  119.3 0.0 collective-permute-done.10.came_ref
  119.3 0.1 shard_map.63
  119.4 0.1 collective-permute-start.13
  119.5 2.0 %collective-permute-start.12 = (f16[32,1152]{1,0:T(8,128)(2,1)S(1)}, f16[32,1152]{1,0:T(8,128)(2,1)S(1)}, u32[]{:S(2)}, u32[]{:S(2)}) collective-permute-start(f16[32,1152]{1,0:T(8,128)(2,1)S(1)} %convert_element_type.44), channel_id=1, source_target_pairs={{0,64},{64,128},{128,192},{192,0},{1,65},{65,129},{129,193},{193,1... | collective-permute-start | bytes 221192 | tf_op jit(solution)/shard_map/ppermute | solution.py:375
  121.5 0.0 collective-permute-done.9
  121.5 2.1 %collective-permute-start.11 = (f16[32,1152]{1,0:T(8,128)(2,1)S(1)}, f16[32,1152]{1,0:T(8,128)(2,1)S(1)}, u32[]{:S(2)}, u32[]{:S(2)}) collective-permute-start(f16[32,1152]{1,0:T(8,128)(2,1)S(1)} %convert_element_type.42), channel_id=1, source_target_pairs={{0,128},{64,192},{128,0},{192,64},{1,129},{65,193},{129,1},{193,65... | collective-permute-start | bytes 221192 | tf_op jit(solution)/shard_map/ppermute | solution.py:375
  123.6 0.5 slice_bitcast_fusion
  124.1 0.0 collective-permute-done.8
  124.2 0.0 collective-permute-done.7
  124.2 0.0 collective-permute-done.13
  124.2 0.5 collective-permute-done.12
  124.7 2.7 %collective-permute-done.11 = f16[32,1152]{1,0:T(8,128)(2,1)S(1)} collective-permute-done((f16[32,1152]{1,0:T(8,128)(2,1)S(1)}, f16[32,1152]{1,0:T(8,128)(2,1)S(1)}, u32[]{:S(2)}, u32[]{:S(2)}) %collective-permute-start.11) | collective-permute-done | bytes 73760 | tf_op jit(solution)/shard_map/ppermute | solution.py:375
  127.4 0.8 shard_map.64
  (13 shorter events, 0.2 us)
Async XLA Ops:
  21.7 7.2 %collective-permute-start.1 = (bf16[256,256]{1,0:T(8,128)(2,1)S(1)}, bf16[256,256]{1,0:T(8,128)(2,1)S(1)}, u32[]{:S(2)}, u32[]{:S(2)}) collective-permute-start(bf16[256,256]{1,0:T(8,128)(2,1)S(1)} %get-tuple-element.35.u0_ref), channel_id=1, source_target_pairs={{0,3},{1,0},{2,1},{3,2},{4,7},{5,4},{6,5},{7,6},{8,11},{9,8},{10,9... | collective-permute-start | bytes 393224 | tf_op jit(solution)/shard_map/ppermute | solution.py:375
  24.5 8.6 %collective-permute-start.5 = (bf16[256,256]{1,0:T(8,128)(2,1)S(1)}, bf16[256,256]{1,0:T(8,128)(2,1)S(1)}, u32[]{:S(2)}, u32[]{:S(2)}) collective-permute-start(bf16[256,256]{1,0:T(8,128)(2,1)S(1)} %get-tuple-element.36.after_ref.u0_ref), channel_id=1, source_target_pairs={{0,3},{1,0},{2,1},{3,2},{4,7},{5,4},{6,5},{7,6},{8,11},{9,8},{10,9... | collective-permute-start | bytes 393224 | tf_op jit(solution)/shard_map/ppermute | solution.py:375
  25.3 7.8 %collective-permute-start.4 = (bf16[256,256]{1,0:T(8,128)(2,1)S(1)}, bf16[256,256]{1,0:T(8,128)(2,1)S(1)}, u32[]{:S(2)}, u32[]{:S(2)}) collective-permute-start(bf16[256,256]{1,0:T(8,128)(2,1)S(1)} %get-tuple-element.36.after_ref.u0_ref), channel_id=1, source_target_pairs={{0,2},{1,3},{2,0},{3,1},{4,6},{5,7},{6,4},{7,5},{8,10},{9,11},{10,... | collective-permute-start | bytes 393224 | tf_op jit(solution)/shard_map/ppermute | solution.py:375
  25.8 8.1 %collective-permute-start.3 = (bf16[256,256]{1,0:T(8,128)(2,1)S(1)}, bf16[256,256]{1,0:T(8,128)(2,1)S(1)}, u32[]{:S(2)}, u32[]{:S(2)}) collective-permute-start(bf16[256,256]{1,0:T(8,128)(2,1)S(1)} %get-tuple-element.36.after_ref.u0_ref), channel_id=1, source_target_pairs={{0,1},{1,2},{2,3},{3,0},{4,5},{5,6},{6,7},{7,4},{8,9},{9,10},{10,1... | collective-permute-start | bytes 393224 | tf_op jit(solution)/shard_map/ppermute | solution.py:375
  26.7 8.6 %collective-permute-start = (bf16[256,256]{1,0:T(8,128)(2,1)S(1)}, bf16[256,256]{1,0:T(8,128)(2,1)S(1)}, u32[]{:S(2)}, u32[]{:S(2)}) collective-permute-start(bf16[256,256]{1,0:T(8,128)(2,1)S(1)} %get-tuple-element.35.u0_ref), channel_id=1, source_target_pairs={{0,1},{1,2},{2,3},{3,0},{4,5},{5,6},{6,7},{7,4},{8,9},{9,10},{10,1... | collective-permute-start | bytes 393224 | tf_op jit(solution)/shard_map/ppermute | solution.py:375
  28.8 6.5 %collective-permute-start.2 = (bf16[256,256]{1,0:T(8,128)(2,1)S(1)}, bf16[256,256]{1,0:T(8,128)(2,1)S(1)}, u32[]{:S(2)}, u32[]{:S(2)}) collective-permute-start(bf16[256,256]{1,0:T(8,128)(2,1)S(1)} %collective-permute-done.1.u3_ref), channel_id=1, source_target_pairs={{0,3},{1,0},{2,1},{3,2},{4,7},{5,4},{6,5},{7,6},{8,11},{9,8},{10,9... | collective-permute-start | bytes 393224 | tf_op jit(solution)/shard_map/ppermute | solution.py:375
  112.3 2.0 %collective-permute-start.6 = (f32[4,32,1024]{2,1,0:T(8,128)S(1)}, f32[4,32,1024]{2,1,0:T(8,128)S(1)}, u32[]{:S(2)}, u32[]{:S(2)}) collective-permute-start(f32[4,32,1024]{2,1,0:T(8,128)S(1)} %get-tuple-element.54), channel_id=1, source_target_pairs={{0,32},{32,0},{1,33},{33,1},{2,34},{34,2},{3,35},{35,3},{4,36},{36... | collective-permute-start | bytes 1572872 | tf_op jit(solution)/shard_map/ppermute | solution.py:379
  113.6 5.7 %collective-permute-start.10 = (f32[4,32,1024]{2,1,0:T(8,128)S(1)}, f32[4,32,1024]{2,1,0:T(8,128)S(1)}, u32[]{:S(2)}, u32[]{:S(2)}) collective-permute-start(f32[4,32,1024]{2,1,0:T(8,128)S(1)} %get-tuple-element.62), channel_id=1, source_target_pairs={{0,32},{32,0},{1,33},{33,1},{2,34},{34,2},{3,35},{35,3},{4,36},{36... | collective-permute-start | bytes 1572872 | tf_op jit(solution)/shard_map/ppermute | solution.py:379
  114.4 7.1 %collective-permute-start.9 = (f16[32,1152]{1,0:T(8,128)(2,1)S(1)}, f16[32,1152]{1,0:T(8,128)(2,1)S(1)}, u32[]{:S(2)}, u32[]{:S(2)}) collective-permute-start(f16[32,1152]{1,0:T(8,128)(2,1)S(1)} %convert_element_type.40), channel_id=1, source_target_pairs={{0,192},{64,0},{128,64},{192,128},{1,193},{65,1},{129,65},{193,129... | collective-permute-start | bytes 221192 | tf_op jit(solution)/shard_map/ppermute | solution.py:375
  115.9 8.2 %collective-permute-start.8 = (f16[32,1152]{1,0:T(8,128)(2,1)S(1)}, f16[32,1152]{1,0:T(8,128)(2,1)S(1)}, u32[]{:S(2)}, u32[]{:S(2)}) collective-permute-start(f16[32,1152]{1,0:T(8,128)(2,1)S(1)} %convert_element_type.38), channel_id=1, source_target_pairs={{0,64},{64,128},{128,192},{192,0},{1,65},{65,129},{129,193},{193,1... | collective-permute-start | bytes 221192 | tf_op jit(solution)/shard_map/ppermute | solution.py:375
  116.6 7.6 %collective-permute-start.7 = (f16[32,1152]{1,0:T(8,128)(2,1)S(1)}, f16[32,1152]{1,0:T(8,128)(2,1)S(1)}, u32[]{:S(2)}, u32[]{:S(2)}) collective-permute-start(f16[32,1152]{1,0:T(8,128)(2,1)S(1)} %convert_element_type.36), channel_id=1, source_target_pairs={{0,128},{64,192},{128,0},{192,64},{1,129},{65,193},{129,1},{193,65... | collective-permute-start | bytes 221192 | tf_op jit(solution)/shard_map/ppermute | solution.py:375
  119.4 4.8 %collective-permute-start.13 = (f16[32,1152]{1,0:T(8,128)(2,1)S(1)}, f16[32,1152]{1,0:T(8,128)(2,1)S(1)}, u32[]{:S(2)}, u32[]{:S(2)}) collective-permute-start(f16[32,1152]{1,0:T(8,128)(2,1)S(1)} %convert_element_type.46), channel_id=1, source_target_pairs={{0,192},{64,0},{128,64},{192,128},{1,193},{65,1},{129,65},{193,129... | collective-permute-start | bytes 221192 | tf_op jit(solution)/shard_map/ppermute | solution.py:375
  119.5 5.2 %collective-permute-start.12 = (f16[32,1152]{1,0:T(8,128)(2,1)S(1)}, f16[32,1152]{1,0:T(8,128)(2,1)S(1)}, u32[]{:S(2)}, u32[]{:S(2)}) collective-permute-start(f16[32,1152]{1,0:T(8,128)(2,1)S(1)} %convert_element_type.44), channel_id=1, source_target_pairs={{0,64},{64,128},{128,192},{192,0},{1,65},{65,129},{129,193},{193,1... | collective-permute-start | bytes 221192 | tf_op jit(solution)/shard_map/ppermute | solution.py:375
  121.5 5.9 %collective-permute-start.11 = (f16[32,1152]{1,0:T(8,128)(2,1)S(1)}, f16[32,1152]{1,0:T(8,128)(2,1)S(1)}, u32[]{:S(2)}, u32[]{:S(2)}) collective-permute-start(f16[32,1152]{1,0:T(8,128)(2,1)S(1)} %convert_element_type.42), channel_id=1, source_target_pairs={{0,128},{64,192},{128,0},{192,64},{1,129},{65,193},{129,1},{193,65... | collective-permute-start | bytes 221192 | tf_op jit(solution)/shard_map/ppermute | solution.py:375
where the time goes:
time: 129 us; the launch traced here: 128 us
  blocking collectives  89 us (69%)
  starting transfers between devices  19.5 us (15%)
  Pallas kernels  14 us (11%)
  waiting for transfers between devices  4.2 us (3%)
    all_to_all x7, blocking collectives, share(): return lax.all_to_all(value, axes, 0, 0, tiled=True)  89 us
    ppermute x12, starting transfers between devices, shift(): return lax.ppermute(value, axis, [(i, (i + step) % 4) for i in range(4)])  18.8 us
    pallas_call x15, Pallas kernels, run(): pl.pallas_call(kernel, out_shape=[shape(o) for o in outs], in_specs=[pl.B...  14 us
    ppermute x12, waiting for transfers between devices, shift(): return lax.ppermute(value, axis, [(i, (i + step) % 4) for i in range(4)])  4.08 us
  transfers between devices with their start and end apart: 14, of which 5 were waited for; matrix products, arithmetic and copies ran while one was open for 0% of the time, Pallas kernels for 3%

commit v1 on v0

--- a/solution.py
+++ b/solution.py
@@ -147,7 +147,8 @@
     u3_ref,
     low_ref,
     mass_ref,
-    scores_ref,
+    weights_ref,
+    product_ref,
     exp_ref,
     unit_t_ref,
     total_ref,
@@ -168,7 +169,7 @@
         for unit_ref, start in zip(units, starts):
             rows = pl.ds(start, BLOCK)
             scores = jnp.dot(unit_ref[...], low, preferred_element_type=f32)
-            scores_ref[rows, cols] = scores
+            product_ref[rows, cols] = weights_ref[rows, cols] * scores
             grown = jnp.exp2(scores * (log2_e / student_temp))
             exp_ref[rows, cols] = grown
             parts_ref[rows, :] += sum(grown[:, t : t + LANES] for t in range(LANES, WIDE, LANES)) + grown[:, :LANES]
@@ -181,7 +182,7 @@
     row_of_lane_sums(parts_ref, put)
 
 
-def scaled_rows(column, weights_ref, parts_ref, scores_ref=None, cross_ref=None):
+def scaled_rows(column, weights_ref, parts_ref, product_ref=None, cross_ref=None):
     scale = [jnp.broadcast_to(column[t : t + 1, :], (8, LANES)) for t in range(COL_TILES)]
 
     for i in range(0, ROWS, 8):
@@ -191,11 +192,11 @@
             cols = pl.ds(t * LANES, LANES)
             term = weights_ref[rows, cols] * scale[t]
             mass = term if mass is None else mass + term
-            if scores_ref is not None:
-                term = term * scores_ref[rows, cols]
+            if product_ref is not None:
+                term = product_ref[rows, cols] * scale[t]
                 cross = term if cross is None else cross + term
         parts_ref[rows, :] = mass
-        if scores_ref is not None:
+        if product_ref is not None:
             cross_ref[rows, :] = cross
 
 
@@ -212,10 +213,10 @@
         pay_ref[k, :, ROWS:FLAT] = owned_piece(extra, k) if spread else extra
 
 
-def last_row_kernel(mass_ref, weights_ref, scores_ref, pay_ref, column_ref, parts_ref, cross_ref, row_ref):
+def last_row_kernel(mass_ref, weights_ref, product_ref, pay_ref, column_ref, parts_ref, cross_ref, row_ref):
     column = 1.0 / jnp.sum(mass_ref[...], axis=0)
     column_ref[...] = column
-    scaled_rows(column, weights_ref, parts_ref, scores_ref, cross_ref)
+    scaled_rows(column, weights_ref, parts_ref, product_ref, cross_ref)
 
     def put_mass(g, row):
         row_ref[g : g + 1, :] = row
@@ -330,17 +331,31 @@
     own_ref[...] = kept_ref[0] + came_ref[0]
 
 
-def sum_kernel(*refs):
-    out_ref = refs[-1]
-    for half in range(2):
-        own_ref, *block_refs = refs[4 * half : 4 * half + 4]
-        scales = [jnp.exp2(ref[0:8, HALF:] - HEAD) for ref in block_refs]
-        for t in range(HALF // LANES):
-            cols = pl.ds(t * LANES, LANES)
-            value = own_ref[:, cols]
-            for ref, scale in zip(block_refs, scales):
-                value = value + ref[:, cols] * scale[t : t + 1, :]
-            out_ref[:, pl.ds(half * HALF + t * LANES, LANES)] = value
+def half_sum(own_ref, block_refs, out_ref):
+    scales = [jnp.exp2(ref[0:8, HALF:] - HEAD) for ref in block_refs]
+    for t in range(HALF // LANES):
+        cols = pl.ds(t * LANES, LANES)
+        value = own_ref[:, cols]
+        for ref, scale in zip(block_refs, scales):
+            value = value + ref[:, cols] * scale[t : t + 1, :]
+        out_ref[:, cols] = value
+
+
+def sum_kernel(own_ref, *refs):
+    half_sum(own_ref, refs[:3], refs[3])
+
+
+def last_sum_kernel(first_ref, own_ref, *refs):
+    out_hbm, second_ref, sems = refs[3:]
+    copies = [
+        pltpu.make_async_copy(ref, out_hbm.at[:, pl.ds(half * HALF, HALF)], sems.at[half])
+        for half, ref in enumerate((first_ref, second_ref))
+    ]
+    copies[0].start()
+    half_sum(own_ref, refs[:3], second_ref)
+    copies[1].start()
+    for copy in copies:
+        copy.wait()
 
 
 def call(kernel, outs, scratch, homes):
@@ -405,9 +420,9 @@
     above = shift(student, 3, "x")
     students = [student, shift(student, 1, "x"), shift(above, 3, "x"), above]
     weights, mass = call(teacher_kernel, [table, inverse_row], [], "vvvvv")(*teachers, low)
-    scores, grown, unit_t, extra, pay = call(
-        student_kernel, [table, table, ((WIDTH, ROWS), bf16, True), crops, to_batch], [lanes], "vvvvvv"
-    )(*students, low, mass)
+    product, grown, unit_t, extra, pay = call(
+        student_kernel, [table, table, ((WIDTH, ROWS), bf16, True), crops, to_batch], [lanes], "vvvvvvv"
+    )(*students, low, mass, weights)
     for iteration in range(ITERS - 1):
         first = iteration == 0
         (pay,) = call(functools.partial(row_kernel, first), [to_proto], [lanes, row], "vvv")(
@@ -424,7 +439,7 @@
         [to_proto, column],
         [lanes, lanes, pltpu.VMEM((2 * ROW_TILES, LANES), f32)],
         "vvv",
-    )(share(pay, BATCH, BATCHES), weights, scores)
+    )(share(pay, BATCH, BATCHES), weights, product)
     part, whole = ((4, 32, HALF), f32, True), ((ROWS, LANES), f32, True)
     tables = (weights, grown, column_scale, unit_t, protos, inverse)
     kept, sent, prob, target, own = call(
@@ -433,7 +448,14 @@
     first = scatter_half(kept, sent)
     kept, sent = call(second_grad_kernel, [part, part], [], "vvvvvvvv")(*tables, prob, target)
     second = scatter_half(kept, sent)
-    (out,) = call(sum_kernel, [((32, COLS), f32, False)], [], "vvvvvvvv")(*first, *second)
+    half = ((32, HALF), f32, True)
+    (first,) = call(sum_kernel, [half], [], "vvvv")(*first)
+    (out,) = call(
+        last_sum_kernel,
+        [((32, COLS), f32, None)],
+        [pltpu.VMEM((32, HALF), f32), pltpu.SemaphoreType.DMA((2,))],
+        "vvvvv",
+    )(first, *second)
     return (out, own[0, :OWN])
 
 

time: 129 us -> 129 us (level)
    pallas_call x15 -> x16, Pallas kernels: 14 us -> 13.9 us  [run(): pl.pallas_call(kernel, out_shape=[shape(o) for o in outs], in_specs=[pl.B...]
  transfers between devices with their start and end apart: 14 -> 14, of which waited for: 5 -> 4; matrix products, arithmetic and copies ran while one was open for 0% -> 1% of each run, Pallas kernels for 3% -> 3%
where the time goes in v1:
time: 129 us; the launch traced here: 128 us
  blocking collectives  89 us (69%)
  starting transfers between devices  19.5 us (15%)
  Pallas kernels  13.9 us (11%)
  waiting for transfers between devices  4.04 us (3%)
    all_to_all x7, blocking collectives, share(): return lax.all_to_all(value, axes, 0, 0, tiled=True)  89 us
    ppermute x12, starting transfers between devices, shift(): return lax.ppermute(value, axis, [(i, (i + step) % 4) for i in range(4)])  18.8 us
    pallas_call x16, Pallas kernels, run(): pl.pallas_call(kernel, out_shape=[shape(o) for o in outs], in_specs=[pl.B...  13.9 us
    ppermute x12, waiting for transfers between devices, shift(): return lax.ppermute(value, axis, [(i, (i + step) % 4) for i in range(4)])  4.03 us
  transfers between devices with their start and end apart: 14, of which 4 were waited for; matrix products, arithmetic and copies ran while one was open for 1% of the time, Pallas kernels for 3%

profile of v1, /device:TPU:8, one launch (start us, length us, event | category | flops | bytes accessed | tf_op | source)
XLA Modules:
  0.0 128.1 jit_solution(1627545456947556397)
XLA Ops:
  0.6 0.9 shard_map.50
  1.5 20.1 %all_to_all.35.came_ref = bf16[8,64,256]{2,1,0:T(8,128)(2,1)S(1)} all-to-all(bf16[8,64,256]{2,1,0:T(8,128)(2,1)S(1)} %shard_map.50), channel_id=1, replica_groups=mesh['y'=4,'core'=2,'z'=8,'x'=4] {'z'}, dimensions={0} | all-to-all | bytes 524288 | tf_op jit(solution)/shard_map/all_to_all | solution.py:386
  21.7 2.8 %collective-permute-start.1 = (bf16[256,256]{1,0:T(8,128)(2,1)S(1)}, bf16[256,256]{1,0:T(8,128)(2,1)S(1)}, u32[]{:S(2)}, u32[]{:S(2)}) collective-permute-start(bf16[256,256]{1,0:T(8,128)(2,1)S(1)} %get-tuple-element.35.u0_ref), channel_id=1, source_target_pairs={{0,3},{1,0},{2,1},{3,2},{4,7},{5,4},{6,5},{7,6},{8,11},{9,8},{10,9... | collective-permute-start | bytes 393224 | tf_op jit(solution)/shard_map/ppermute | solution.py:390
  24.5 0.8 collective-permute-start.5
  25.3 0.5 collective-permute-start.4
  25.8 0.9 collective-permute-start.3
  26.7 2.1 %collective-permute-start = (bf16[256,256]{1,0:T(8,128)(2,1)S(1)}, bf16[256,256]{1,0:T(8,128)(2,1)S(1)}, u32[]{:S(2)}, u32[]{:S(2)}) collective-permute-start(bf16[256,256]{1,0:T(8,128)(2,1)S(1)} %get-tuple-element.35.u0_ref), channel_id=1, source_target_pairs={{0,1},{1,2},{2,3},{3,0},{4,5},{5,6},{6,7},{7,4},{8,9},{9,10},{10,1... | collective-permute-start | bytes 393224 | tf_op jit(solution)/shard_map/ppermute | solution.py:390
  28.8 0.0 collective-permute-done.1.u3_ref
  28.8 2.6 %collective-permute-start.2 = (bf16[256,256]{1,0:T(8,128)(2,1)S(1)}, bf16[256,256]{1,0:T(8,128)(2,1)S(1)}, u32[]{:S(2)}, u32[]{:S(2)}) collective-permute-start(bf16[256,256]{1,0:T(8,128)(2,1)S(1)} %collective-permute-done.1.u3_ref), channel_id=1, source_target_pairs={{0,3},{1,0},{2,1},{3,2},{4,7},{5,4},{6,5},{7,6},{8,11},{9,8},{10,9... | collective-permute-start | bytes 393224 | tf_op jit(solution)/shard_map/ppermute | solution.py:390
  31.5 1.6 %shard_map.52 = (bf16[256,2048]{1,0:T(8,128)(2,1)S(1)}, f32[1,2048]{1,0:T(1,128)S(1)}, f32[256,2048]{1,0:T(8,128)S(1)}) custom-call(f32[256,2048]{1,0:T(8,128)} %proto_hbm.1, bf16[256,256]{1,0:T(8,128)(2,1)S(1)} %get-tuple-element.36.after_ref.u0_ref), custom_call_target="tpu_custom_call" | custom-call | tf_op jit(solution)/shard_map/pallas_call | solution.py:372
  33.1 0.0 collective-permute-done.5.u3_ref
  33.1 0.0 collective-permute-done.4.u2_ref
  33.1 0.8 collective-permute-done.3.u1_ref
  33.9 1.3 shard_map.53
  35.2 0.1 collective-permute-done.u1_ref
  35.3 0.0 collective-permute-done.2.u2_ref
  35.3 2.1 %shard_map.54 = (f32[1024,2048]{1,0:T(8,128)S(1)}, f32[1024,2048]{1,0:T(8,128)S(1)}, bf16[256,1024]{1,0:T(8,128)(2,1)S(1)}, f32[8,128]{1,0:T(8,128)S(1)}, f32[8,16,128]{2,1,0:T(8,128)S(1)}) custom-call(bf16[256,256]{1,0:T(8,128)(2,1)S(1)} %get-tuple-element.35.u0_ref, bf16[256,256]{1,0:T(8,128)(2,1)S(1)} %collective-permute-done.u1_ref, ...), custom_call_target="tpu_custom_call" | custom-call | tf_op jit(solution)/shard_map/pallas_call | solution.py:372
  37.4 8.9 %all_to_all.36.mass_ref = f32[8,16,128]{2,1,0:T(8,128)S(1)} all-to-all(f32[8,16,128]{2,1,0:T(8,128)S(1)} %get-tuple-element.40), channel_id=1, replica_groups=mesh['y'=4,'core'=2,'z'=8,'x'=4] {'y','core'}, dimensions={0} | all-to-all | bytes 131072 | tf_op jit(solution)/shard_map/all_to_all | solution.py:386
  46.3 0.7 shard_map.55
  47.0 15.9 %all_to_all.37.mass_ref = f32[32,1,1152]{2,1,0:T(1,128)S(1)} all-to-all(f32[32,1,1152]{2,1,0:T(1,128)S(1)} %shard_map.55), channel_id=1, replica_groups=mesh['y'=4,'core'=2,'z'=8,'x'=4] {'z','x'}, dimensions={0} | all-to-all | bytes 294912 | tf_op jit(solution)/shard_map/all_to_all | solution.py:386
  62.9 0.8 shard_map.56
  63.7 8.0 %all_to_all.38.mass_ref = f32[8,16,128]{2,1,0:T(8,128)S(1)} all-to-all(f32[8,16,128]{2,1,0:T(8,128)S(1)} %get-tuple-element.42), channel_id=1, replica_groups=mesh['y'=4,'core'=2,'z'=8,'x'=4] {'y','core'}, dimensions={0} | all-to-all | bytes 131072 | tf_op jit(solution)/shard_map/all_to_all | solution.py:386
  71.7 0.6 shard_map.57
  72.4 14.0 %all_to_all.39.mass_ref = f32[32,1,1152]{2,1,0:T(1,128)S(1)} all-to-all(f32[32,1,1152]{2,1,0:T(1,128)S(1)} %shard_map.57), channel_id=1, replica_groups=mesh['y'=4,'core'=2,'z'=8,'x'=4] {'z','x'}, dimensions={0} | all-to-all | bytes 294912 | tf_op jit(solution)/shard_map/all_to_all | solution.py:386
  86.4 0.8 shard_map.58
  87.2 8.0 %all_to_all.40.mass_ref = f32[8,16,128]{2,1,0:T(8,128)S(1)} all-to-all(f32[8,16,128]{2,1,0:T(8,128)S(1)} %get-tuple-element.44), channel_id=1, replica_groups=mesh['y'=4,'core'=2,'z'=8,'x'=4] {'y','core'}, dimensions={0} | all-to-all | bytes 131072 | tf_op jit(solution)/shard_map/all_to_all | solution.py:386
  95.2 1.3 %shard_map.59 = (f32[32,1,1152]{2,1,0:T(1,128)S(1)}, f32[16,128]{1,0:T(8,128)S(1)}) custom-call(f32[8,16,128]{2,1,0:T(8,128)S(1)} %all_to_all.40.mass_ref, f32[1024,2048]{1,0:T(8,128)S(1)} %get-tuple-element.39.weights_ref.refs_0_, f32[1024,2048]{1,0:T(8,128)S(1)} %get-tuple-element.45.product_ref), custom_call_target="tpu_custom_call" | custom-call | tf_op jit(solution)/shard_map/pallas_call | solution.py:372
  96.5 14.0 %all_to_all.41.mass_ref = f32[32,1,1152]{2,1,0:T(1,128)S(1)} all-to-all(f32[32,1,1152]{2,1,0:T(1,128)S(1)} %get-tuple-element.46), channel_id=1, replica_groups=mesh['y'=4,'core'=2,'z'=8,'x'=4] {'z','x'}, dimensions={0} | all-to-all | bytes 294912 | tf_op jit(solution)/shard_map/all_to_all | solution.py:386
  110.5 1.6 %shard_map.60 = (f32[4,32,1024]{2,1,0:T(8,128)S(1)}, f32[4,32,1024]{2,1,0:T(8,128)S(1)}, f32[1024,128]{1,0:T(8,128)S(1)}, f32[1024,128]{1,0:T(8,128)S(1)}, f32[1,128]{1,0:T(1,128)S(1)}) custom-call(f32[32,1,1152]{2,1,0:T(1,128)S(1)} %all_to_all.41.mass_ref, f32[8,128]{1,0:T(8,128)S(1)} %get-tuple-element.47.total_ref, ...), custom_call_target="tpu_custom_call" | custom-call | tf_op jit(solution)/shard_map/pallas_call | solution.py:372
  112.1 0.1 collective-permute-start.6
  112.2 1.3 %shard_map.63 = (f32[4,32,1024]{2,1,0:T(8,128)S(1)}, f32[4,32,1024]{2,1,0:T(8,128)S(1)}) custom-call(f32[1024,2048]{1,0:T(8,128)S(1)} %get-tuple-element.39.weights_ref.refs_0_, f32[1024,2048]{1,0:T(8,128)S(1)} %get-tuple-element.48.exp_ref.refs_1_, f32[16,128]{1,0:T(8,128)S(1)} %get-tuple-element.49.column_ref.refs_2_, ...), custom_call_target="tpu_custom_call" | custom-call | tf_op jit(solution)/shard_map/pallas_call | solution.py:372
  113.5 0.6 collective-permute-start.10
  114.1 0.0 collective-permute-done.6.came_ref
  114.1 0.1 shard_map.61
  114.2 1.5 %collective-permute-start.9 = (f16[32,1152]{1,0:T(8,128)(2,1)S(1)}, f16[32,1152]{1,0:T(8,128)(2,1)S(1)}, u32[]{:S(2)}, u32[]{:S(2)}) collective-permute-start(f16[32,1152]{1,0:T(8,128)(2,1)S(1)} %convert_element_type.40), channel_id=1, source_target_pairs={{0,192},{64,0},{128,64},{192,128},{1,193},{65,1},{129,65},{193,129... | collective-permute-start | bytes 221192 | tf_op jit(solution)/shard_map/ppermute | solution.py:390
  115.8 0.6 collective-permute-start.8
  116.4 2.7 %collective-permute-start.7 = (f16[32,1152]{1,0:T(8,128)(2,1)S(1)}, f16[32,1152]{1,0:T(8,128)(2,1)S(1)}, u32[]{:S(2)}, u32[]{:S(2)}) collective-permute-start(f16[32,1152]{1,0:T(8,128)(2,1)S(1)} %convert_element_type.36), channel_id=1, source_target_pairs={{0,128},{64,192},{128,0},{192,64},{1,129},{65,193},{129,1},{193,65... | collective-permute-start | bytes 221192 | tf_op jit(solution)/shard_map/ppermute | solution.py:390
  119.1 0.0 collective-permute-done.10.came_ref
  119.1 0.1 shard_map.64
  119.3 0.1 collective-permute-start.13
  119.3 2.0 %collective-permute-start.12 = (f16[32,1152]{1,0:T(8,128)(2,1)S(1)}, f16[32,1152]{1,0:T(8,128)(2,1)S(1)}, u32[]{:S(2)}, u32[]{:S(2)}) collective-permute-start(f16[32,1152]{1,0:T(8,128)(2,1)S(1)} %convert_element_type.44), channel_id=1, source_target_pairs={{0,64},{64,128},{128,192},{192,0},{1,65},{65,129},{129,193},{193,1... | collective-permute-start | bytes 221192 | tf_op jit(solution)/shard_map/ppermute | solution.py:390
  121.4 0.0 collective-permute-done.9
  121.4 2.1 %collective-permute-start.11 = (f16[32,1152]{1,0:T(8,128)(2,1)S(1)}, f16[32,1152]{1,0:T(8,128)(2,1)S(1)}, u32[]{:S(2)}, u32[]{:S(2)}) collective-permute-start(f16[32,1152]{1,0:T(8,128)(2,1)S(1)} %convert_element_type.42), channel_id=1, source_target_pairs={{0,128},{64,192},{128,0},{192,64},{1,129},{65,193},{129,1},{193,65... | collective-permute-start | bytes 221192 | tf_op jit(solution)/shard_map/ppermute | solution.py:390
  123.4 0.5 slice_bitcast_fusion
  124.0 0.0 collective-permute-done.8
  124.0 0.0 collective-permute-done.7
  124.1 0.0 collective-permute-done.13
  124.1 0.4 collective-permute-done.12
  124.6 2.7 %collective-permute-done.11 = f16[32,1152]{1,0:T(8,128)(2,1)S(1)} collective-permute-done((f16[32,1152]{1,0:T(8,128)(2,1)S(1)}, f16[32,1152]{1,0:T(8,128)(2,1)S(1)}, u32[]{:S(2)}, u32[]{:S(2)}) %collective-permute-start.11) | collective-permute-done | bytes 73760 | tf_op jit(solution)/shard_map/ppermute | solution.py:390
  127.2 0.7 shard_map.65
  (14 shorter events, 0.2 us)
Async XLA Ops:
  21.7 7.2 %collective-permute-start.1 = (bf16[256,256]{1,0:T(8,128)(2,1)S(1)}, bf16[256,256]{1,0:T(8,128)(2,1)S(1)}, u32[]{:S(2)}, u32[]{:S(2)}) collective-permute-start(bf16[256,256]{1,0:T(8,128)(2,1)S(1)} %get-tuple-element.35.u0_ref), channel_id=1, source_target_pairs={{0,3},{1,0},{2,1},{3,2},{4,7},{5,4},{6,5},{7,6},{8,11},{9,8},{10,9... | collective-permute-start | bytes 393224 | tf_op jit(solution)/shard_map/ppermute | solution.py:390
  24.5 8.6 %collective-permute-start.5 = (bf16[256,256]{1,0:T(8,128)(2,1)S(1)}, bf16[256,256]{1,0:T(8,128)(2,1)S(1)}, u32[]{:S(2)}, u32[]{:S(2)}) collective-permute-start(bf16[256,256]{1,0:T(8,128)(2,1)S(1)} %get-tuple-element.36.after_ref.u0_ref), channel_id=1, source_target_pairs={{0,3},{1,0},{2,1},{3,2},{4,7},{5,4},{6,5},{7,6},{8,11},{9,8},{10,9... | collective-permute-start | bytes 393224 | tf_op jit(solution)/shard_map/ppermute | solution.py:390
  25.3 7.8 %collective-permute-start.4 = (bf16[256,256]{1,0:T(8,128)(2,1)S(1)}, bf16[256,256]{1,0:T(8,128)(2,1)S(1)}, u32[]{:S(2)}, u32[]{:S(2)}) collective-permute-start(bf16[256,256]{1,0:T(8,128)(2,1)S(1)} %get-tuple-element.36.after_ref.u0_ref), channel_id=1, source_target_pairs={{0,2},{1,3},{2,0},{3,1},{4,6},{5,7},{6,4},{7,5},{8,10},{9,11},{10,... | collective-permute-start | bytes 393224 | tf_op jit(solution)/shard_map/ppermute | solution.py:390
  25.8 8.1 %collective-permute-start.3 = (bf16[256,256]{1,0:T(8,128)(2,1)S(1)}, bf16[256,256]{1,0:T(8,128)(2,1)S(1)}, u32[]{:S(2)}, u32[]{:S(2)}) collective-permute-start(bf16[256,256]{1,0:T(8,128)(2,1)S(1)} %get-tuple-element.36.after_ref.u0_ref), channel_id=1, source_target_pairs={{0,1},{1,2},{2,3},{3,0},{4,5},{5,6},{6,7},{7,4},{8,9},{9,10},{10,1... | collective-permute-start | bytes 393224 | tf_op jit(solution)/shard_map/ppermute | solution.py:390
  26.7 8.6 %collective-permute-start = (bf16[256,256]{1,0:T(8,128)(2,1)S(1)}, bf16[256,256]{1,0:T(8,128)(2,1)S(1)}, u32[]{:S(2)}, u32[]{:S(2)}) collective-permute-start(bf16[256,256]{1,0:T(8,128)(2,1)S(1)} %get-tuple-element.35.u0_ref), channel_id=1, source_target_pairs={{0,1},{1,2},{2,3},{3,0},{4,5},{5,6},{6,7},{7,4},{8,9},{9,10},{10,1... | collective-permute-start | bytes 393224 | tf_op jit(solution)/shard_map/ppermute | solution.py:390
  28.8 6.5 %collective-permute-start.2 = (bf16[256,256]{1,0:T(8,128)(2,1)S(1)}, bf16[256,256]{1,0:T(8,128)(2,1)S(1)}, u32[]{:S(2)}, u32[]{:S(2)}) collective-permute-start(bf16[256,256]{1,0:T(8,128)(2,1)S(1)} %collective-permute-done.1.u3_ref), channel_id=1, source_target_pairs={{0,3},{1,0},{2,1},{3,2},{4,7},{5,4},{6,5},{7,6},{8,11},{9,8},{10,9... | collective-permute-start | bytes 393224 | tf_op jit(solution)/shard_map/ppermute | solution.py:390
  112.1 2.0 %collective-permute-start.6 = (f32[4,32,1024]{2,1,0:T(8,128)S(1)}, f32[4,32,1024]{2,1,0:T(8,128)S(1)}, u32[]{:S(2)}, u32[]{:S(2)}) collective-permute-start(f32[4,32,1024]{2,1,0:T(8,128)S(1)} %get-tuple-element.54), channel_id=1, source_target_pairs={{0,32},{32,0},{1,33},{33,1},{2,34},{34,2},{3,35},{35,3},{4,36},{36... | collective-permute-start | bytes 1572872 | tf_op jit(solution)/shard_map/ppermute | solution.py:394
  113.5 5.6 %collective-permute-start.10 = (f32[4,32,1024]{2,1,0:T(8,128)S(1)}, f32[4,32,1024]{2,1,0:T(8,128)S(1)}, u32[]{:S(2)}, u32[]{:S(2)}) collective-permute-start(f32[4,32,1024]{2,1,0:T(8,128)S(1)} %get-tuple-element.62), channel_id=1, source_target_pairs={{0,32},{32,0},{1,33},{33,1},{2,34},{34,2},{3,35},{35,3},{4,36},{36... | collective-permute-start | bytes 1572872 | tf_op jit(solution)/shard_map/ppermute | solution.py:394
  114.2 7.1 %collective-permute-start.9 = (f16[32,1152]{1,0:T(8,128)(2,1)S(1)}, f16[32,1152]{1,0:T(8,128)(2,1)S(1)}, u32[]{:S(2)}, u32[]{:S(2)}) collective-permute-start(f16[32,1152]{1,0:T(8,128)(2,1)S(1)} %convert_element_type.40), channel_id=1, source_target_pairs={{0,192},{64,0},{128,64},{192,128},{1,193},{65,1},{129,65},{193,129... | collective-permute-start | bytes 221192 | tf_op jit(solution)/shard_map/ppermute | solution.py:390
  115.8 8.2 %collective-permute-start.8 = (f16[32,1152]{1,0:T(8,128)(2,1)S(1)}, f16[32,1152]{1,0:T(8,128)(2,1)S(1)}, u32[]{:S(2)}, u32[]{:S(2)}) collective-permute-start(f16[32,1152]{1,0:T(8,128)(2,1)S(1)} %convert_element_type.38), channel_id=1, source_target_pairs={{0,64},{64,128},{128,192},{192,0},{1,65},{65,129},{129,193},{193,1... | collective-permute-start | bytes 221192 | tf_op jit(solution)/shard_map/ppermute | solution.py:390
  116.4 7.6 %collective-permute-start.7 = (f16[32,1152]{1,0:T(8,128)(2,1)S(1)}, f16[32,1152]{1,0:T(8,128)(2,1)S(1)}, u32[]{:S(2)}, u32[]{:S(2)}) collective-permute-start(f16[32,1152]{1,0:T(8,128)(2,1)S(1)} %convert_element_type.36), channel_id=1, source_target_pairs={{0,128},{64,192},{128,0},{192,64},{1,129},{65,193},{129,1},{193,65... | collective-permute-start | bytes 221192 | tf_op jit(solution)/shard_map/ppermute | solution.py:390
  119.3 4.8 %collective-permute-start.13 = (f16[32,1152]{1,0:T(8,128)(2,1)S(1)}, f16[32,1152]{1,0:T(8,128)(2,1)S(1)}, u32[]{:S(2)}, u32[]{:S(2)}) collective-permute-start(f16[32,1152]{1,0:T(8,128)(2,1)S(1)} %convert_element_type.46), channel_id=1, source_target_pairs={{0,192},{64,0},{128,64},{192,128},{1,193},{65,1},{129,65},{193,129... | collective-permute-start | bytes 221192 | tf_op jit(solution)/shard_map/ppermute | solution.py:390
  119.3 5.2 %collective-permute-start.12 = (f16[32,1152]{1,0:T(8,128)(2,1)S(1)}, f16[32,1152]{1,0:T(8,128)(2,1)S(1)}, u32[]{:S(2)}, u32[]{:S(2)}) collective-permute-start(f16[32,1152]{1,0:T(8,128)(2,1)S(1)} %convert_element_type.44), channel_id=1, source_target_pairs={{0,64},{64,128},{128,192},{192,0},{1,65},{65,129},{129,193},{193,1... | collective-permute-start | bytes 221192 | tf_op jit(solution)/shard_map/ppermute | solution.py:390
  121.4 5.9 %collective-permute-start.11 = (f16[32,1152]{1,0:T(8,128)(2,1)S(1)}, f16[32,1152]{1,0:T(8,128)(2,1)S(1)}, u32[]{:S(2)}, u32[]{:S(2)}) collective-permute-start(f16[32,1152]{1,0:T(8,128)(2,1)S(1)} %convert_element_type.42), channel_id=1, source_target_pairs={{0,128},{64,192},{128,0},{192,64},{1,129},{65,193},{129,1},{193,65... | collective-permute-start | bytes 221192 | tf_op jit(solution)/shard_map/ppermute | solution.py:390
